TPU v7x, 256 devices: a whole 4x4x8 slice. The times are simulated.
256 devices in a mesh: ctx: 32 (over z_lo, x, core), head: 8 (over z_hi, y).
Axes of the slice: x: 4, y: 4, z: 8 (z_hi: 2, z_lo: 4; z = z_hi * 4 + z_lo), core: 2. Of those that a mesh axis runs over, the one named last changes fastest.
Arguments:
- rotated_query_rows: bfloat16 [32768, 4096], P(('ctx', 'head')), may hold values from -6.5 to 6.5
- rotated_key_rows: bfloat16 [32768, 1024], P(('ctx', 'head')), may hold values from -4 to 4
- value_row_matrix: bfloat16 [32768, 1024], P(('ctx', 'head')), may hold values from -5 to 5
- vert_blocks: int32 [8, 512, 8], P('head', 'ctx'), may hold values from -1 to 495, as said below
- slash_offsets: int32 [8, 512, 4], P('head', 'ctx'), may hold values from -1 to 15, as said below
- out_weight: bfloat16 [4096, 4096], P('head'), may hold values from -0.09375 to 0.09375
- residual: bfloat16 [32768, 4096], P(('ctx', 'head')), may hold values from -0.29882812 to 0.29882812
- norm_gain: bfloat16 [4096], replicated, may hold values from 0.5 to 1.5
Outputs:
- hidden_out: bfloat16 [32768, 4096], P(('ctx', 'head'))
- normed: bfloat16 [32768, 4096], P(('ctx', 'head'))
Inputs may be any that keep to these rules, and one draw needn't show every extreme that they name: `vert_blocks`: for query block i and key-value head h: -1 marks an empty entry; the other entries are distinct key blocks; block 0 is listed when i >= 16, block i - 16 when i > 16, and the others lie in 1 to i - 16. `slash_offsets`: for query block i: the first entry is 0; the others are -1 or distinct offsets of 1 to min(15, i).
All inputs are finite; a program needn't handle non-finite values.
Results may differ from a plain program's by a relative error of at most 0.017.
Values may be sent and summed in bfloat16 or wider, within the bound.
A program may use at most 128 MiB of HBM per device.

v0:
```python
import jax
import jax.numpy as jnp
from jax import lax
from jax.sharding import PartitionSpec as P

QUERY_HEADS = 32
KEY_VALUE_HEADS = 8
HEAD_SIZE = 128
MASK_BLOCK_SIZE = 64


def attend_head(query_blocks, key_head, value_head, vert_list, slash_list, block_ids):
    count_blocks = query_blocks.shape[0]
    slash_blocks = jnp.where(slash_list >= 0, block_ids[:, None] - slash_list, -1)
    listed = jnp.concatenate([vert_list, slash_blocks], axis=1)
    present = listed >= 0
    clamped = jnp.maximum(listed, 0)
    offsets = jnp.arange(MASK_BLOCK_SIZE, dtype=jnp.int32)
    key_rows = (clamped[:, :, None] * MASK_BLOCK_SIZE + offsets[None, None, :]).reshape(
        count_blocks, -1
    )
    key_sel = key_head[key_rows]
    value_sel = value_head[key_rows]
    query_pos = block_ids[:, None] * MASK_BLOCK_SIZE + offsets[None, :]
    allowed = jnp.repeat(present, MASK_BLOCK_SIZE, axis=1)[:, None, :] & (
        key_rows[:, None, :] <= query_pos[:, :, None]
    )
    scores = jnp.einsum(
        "nbgd,nkd->ngbk", query_blocks, key_sel, preferred_element_type=jnp.float32
    ) * HEAD_SIZE ** (-0.5)
    scores = jnp.where(allowed[:, None, :, :], scores, -1e30)
    row_max = jnp.max(scores, axis=-1, keepdims=True)
    weights = jnp.where(allowed[:, None, :, :], jnp.exp(scores - row_max), 0.0)
    total = jnp.sum(weights, axis=-1)
    weights_b = weights.astype(jnp.bfloat16)
    mixed = jnp.einsum("ngbk,nkd->ngbd", weights_b, value_sel, preferred_element_type=jnp.float32)
    mixed = mixed / total[..., None]
    return jnp.transpose(mixed, (0, 2, 1, 3)).astype(jnp.bfloat16)


def per_device(
    rotated_query_rows,
    rotated_key_rows,
    value_row_matrix,
    vert_blocks,
    slash_offsets,
    out_weight,
    residual,
    norm_gain,
):
    query_head, key_local, value_local = (
        lax.all_to_all(rotated_query_rows, "head", split_axis=1, concat_axis=0, tiled=True),
        lax.all_to_all(rotated_key_rows, "head", split_axis=1, concat_axis=0, tiled=True),
        lax.all_to_all(value_row_matrix, "head", split_axis=1, concat_axis=0, tiled=True),
    )
    stretch_rows = query_head.shape[0]
    kv_width = key_local.shape[1]
    heads_kv = kv_width // HEAD_SIZE
    head_group = QUERY_HEADS // KEY_VALUE_HEADS
    full_key_rows, full_value_rows = (
        lax.all_gather(key_local, "ctx", axis=0, tiled=True),
        lax.all_gather(value_local, "ctx", axis=0, tiled=True),
    )
    count_blocks = stretch_rows // MASK_BLOCK_SIZE
    block_ids = lax.axis_index("ctx") * count_blocks + jnp.arange(count_blocks, dtype=jnp.int32)
    query_split = query_head.reshape(count_blocks, MASK_BLOCK_SIZE, heads_kv, head_group, HEAD_SIZE)
    pieces = [
        attend_head(
            query_split[:, :, 0],
            full_key_rows,
            full_value_rows,
            vert_blocks[0],
            slash_offsets[0],
            block_ids,
        )
    ]
    attn = jnp.stack(pieces, axis=2).reshape(stretch_rows, heads_kv * head_group * HEAD_SIZE)
    partial_out = jnp.dot(attn, out_weight, preferred_element_type=jnp.float32).astype(jnp.bfloat16)
    summed = lax.psum_scatter(partial_out, "head", scatter_dimension=0, tiled=True).astype(
        jnp.float32
    )
    stream = residual.astype(jnp.float32) + summed
    hidden_out = stream.astype(jnp.bfloat16)
    mean_square = jnp.mean(stream * stream, axis=-1, keepdims=True)
    normed = (stream * lax.rsqrt(mean_square + 1e-05) * norm_gain.astype(jnp.float32)).astype(
        jnp.bfloat16
    )
    return (hidden_out, normed)


def solution(mesh):
    return jax.shard_map(
        per_device,
        mesh=mesh,
        in_specs=(
            P(("ctx", "head"), None),
            P(("ctx", "head"), None),
            P(("ctx", "head"), None),
            P("head", "ctx", None),
            P("head", "ctx", None),
            P("head", None),
            P(("ctx", "head"), None),
            P(),
        ),
        out_specs=(P(("ctx", "head"), None), P(("ctx", "head"), None)),
        check_vma=False,
    )
```

profile of v0, /device:TPU:1, one launch (start us, length us, event | category | flops | bytes accessed | tf_op | source)
XLA Modules:
  0.0 437.0 jit_solution(15042528849649295543)
XLA Ops:
  7.2 0.0 copy-start
  7.2 0.0 copy-start.5
  7.2 0.0 copy-start.3
  7.2 0.0 all-gather.3.cloned.1.call-start
  7.2 0.9 copy-done
  8.2 21.6 %all_to_all.54 = bf16[128,8,128]{2,0,1:T(8,128)(2,1)} all-to-all(bf16[128,8,128]{2,0,1:T(8,128)(2,1)S(1)} %copy_bitcast_fusion.2), channel_id=1, replica_groups=mesh['ctx'=32,'head'=8] {'head'}, dimensions={1} | all-to-all | bytes 524288 | tf_op jit(solution)/shard_map/all_to_all | solution.py:53
  29.8 0.0 all-gather.3.cloned.1.call-update
  29.8 0.0 all-gather.5.cloned.1.call-start
  29.9 1.0 copy_bitcast_fusion.1
  30.9 13.0 %all_to_all.55 = bf16[128,8,128]{2,0,1:T(8,128)(2,1)} all-to-all(bf16[128,8,128]{2,0,1:T(8,128)(2,1)S(1)} %copy_bitcast_fusion.1), channel_id=1, replica_groups=mesh['ctx'=32,'head'=8] {'head'}, dimensions={1} | all-to-all | bytes 524288 | tf_op jit(solution)/shard_map/all_to_all | solution.py:54
  43.9 0.0 all-gather.5.cloned.1.call-update
  44.0 2.3 copy.36
  46.3 3.6 all-to-all-start.1
  49.8 0.0 reduce-scatter.2.cloned.1.call-start
  49.9 0.0 copy-done.5
  49.9 0.0 copy-done.3
  49.9 0.1 copy.15
  50.0 0.1 add.100
  50.1 0.1 add.101
  50.2 0.1 add.109
  50.3 0.1 add.103
  50.4 0.1 copy.14
  50.5 0.1 broadcast_in_dim.40
  50.6 0.1 and.15
  50.7 0.1 iota_add_fusion
  50.8 1.6 compare_and_fusion
  52.4 33.5 %all-to-all-done.1 = bf16[128,8,512]{2,0,1:T(8,128)(2,1)S(1)} async-done(((bf16[128,8,512]{2,0,1:T(8,128)(2,1)}), bf16[128,8,512]{2,0,1:T(8,128)(2,1)S(1)}, u32[]{:S(2)}, u32[]{:S(2)}) %all-to-all-start.1) | async-done | bytes 1048608 | tf_op jit(solution)/shard_map/all_to_all | solution.py:52
  86.0 1.1 squeeze_reshape.3
  87.1 33.5 %all-gather.3.cloned.1.call-done = bf16[32768,128]{1,0:T(8,128)(2,1)} async-done(((bf16[1024,128]{1,0:T(8,128)(2,1)}), bf16[32768,128]{1,0:T(8,128)(2,1)}) %all-gather.3.cloned.1.call-update) | async-done | bytes 8388624 | tf_op jit(solution)/shard_map/all_gather | solution.py:61
  120.5 45.9 %gather_fusion = bf16[12288,128]{1,0:T(8,128)(2,1)} fusion(bf16[32768,128]{1,0:T(8,128)(2,1)} %all-gather.3.cloned.1.call-done, s32[12288]{0:T(1024)S(1)} %broadcast_clamp_fusion), kind=kCustom, calls=%fused_computation | custom fusion | bytes 6340608 | tf_op jit(solution)/shard_map/gather | solution.py:22
  166.4 4.0 fusion.13
  170.4 9.5 %fusion.19 = (f32[16,4,64]{2,1,0:T(4,128)S(1)}, bf16[16,4,64,768]{3,2,1,0:T(8,128)(2,1)}) fusion(f32[16,768,64,4]{1,2,3,0:T(8,128)S(1)} %fusion.13, pred[16,64,768]{2,1,0:T(8,128)(4,1)} %compare_and_fusion), kind=kOutput, calls=%fused_computation.41 | output fusion | flops 25166592 | bytes 19677184 | tf_op jit(solution)/shard_map/sub | solution.py:33
  179.9 11.0 %all-gather.5.cloned.1.call-done = bf16[32768,128]{1,0:T(8,128)(2,1)} async-done(((bf16[1024,128]{1,0:T(8,128)(2,1)}), bf16[32768,128]{1,0:T(8,128)(2,1)}) %all-gather.5.cloned.1.call-update) | async-done | bytes 8388624 | tf_op jit(solution)/shard_map/all_gather | solution.py:62
  190.9 37.2 %gather_fusion.1 = bf16[12288,128]{1,0:T(8,128)(2,1)S(1)} fusion(bf16[32768,128]{1,0:T(8,128)(2,1)} %all-gather.5.cloned.1.call-done, s32[12288]{0:T(1024)S(1)} %broadcast_clamp_fusion), kind=kCustom, calls=%fused_computation.1 | custom fusion | bytes 6340608 | tf_op jit(solution)/shard_map/gather | solution.py:23
  228.0 0.0 copy-start.6
  228.0 4.7 %fusion.7 = bf16[16,64,4,128]{3,1,2,0:T(8,128)(2,1)S(1)} fusion(bf16[16,768,128,1]{2,1,3,0:T(8,128)(2,1)S(1)} %bitcast.68, bf16[16,4,64,768]{3,2,1,0:T(8,128)(2,1)} %get-tuple-element.5, f32[16,64,4]{1,2,0:T(4,128)S(1)} %bitcast.75), kind=kOutput, calls=%fused_computation.14 | convolution fusion | flops 806354944 | bytes 10502144 | tf_op jit(solution)/shard_map/ngbk,nkd->ngbd/dot_general | solution.py:36
  232.8 0.9 copy.20
  233.7 0.0 copy-done.6
  233.7 6.9 %convolution_convert_fusion = bf16[1024,4096]{1,0:T(8,128)(2,1)} fusion(bf16[512,4096]{1,0:T(8,128)(2,1)S(1)} %copy-done.6, bf16[128,8,4,128]{3,2,1,0:T(4,128)(2,1)S(1)} %bitcast.70), kind=kOutput, calls=%fused_computation.6 | convolution fusion | flops 4299161600 | bytes 13631488 | tf_op jit(solution)/shard_map/dot_general | solution.py:78
  240.6 0.0 copy-start.4
  240.6 0.0 copy-start.2
  240.6 0.0 reduce-scatter.2.cloned.1.call-update
  240.6 0.7 copy-done.4
  241.3 184.5 %reduce-scatter.2.cloned.1.call-done = bf16[128,4096]{1,0:T(8,128)(2,1)} async-done(((bf16[1024,4096]{1,0:T(8,128)(2,1)}), bf16[128,4096]{1,0:T(8,128)(2,1)}) %reduce-scatter.2.cloned.1.call-update) | async-done | bytes 1048592 | tf_op jit(solution)/shard_map/reduce_scatter | solution.py:79
  425.7 0.0 copy-done.2
  425.7 1.6 multiply_reduce_fusion
  427.4 3.0 multiply_convert_fusion
  430.4 0.0 copy-done.1
  (13 shorter events, 0.1 us)
Async XLA Ops:
  7.2 1.0 copy-start
  7.2 42.7 %copy-start.5 = (s32[1,16,4]{1,2,0:T(4,128)S(1)}, s32[1,16,4]{1,2,0:T(4,128)}, u32[]{:S(2)}) copy-start(s32[1,16,4]{1,2,0:T(4,128)} %param.12) | copy-start | bytes 772
  7.2 42.7 %copy-start.3 = (s32[1,16,8]{1,2,0:T(8,128)S(1)}, s32[1,16,8]{1,2,0:T(8,128)}, u32[]{:S(2)}) copy-start(s32[1,16,8]{1,2,0:T(8,128)} %param.11) | copy-start | bytes 1540
  7.2 113.3 %all-gather.3.cloned.1.call-start = ((), (), s32[]{:S(2)}) async-start(), calls=%async_computation.4 | async-start | bytes 8650752 | tf_op jit(solution)/shard_map/all_gather | solution.py:61
  29.8 161.0 %all-gather.5.cloned.1.call-start = ((), (), s32[]{:S(2)}) async-start(), calls=%async_computation.5 | async-start | bytes 8650752 | tf_op jit(solution)/shard_map/all_gather | solution.py:62
  46.3 39.7 %all-to-all-start.1 = ((bf16[128,8,512]{2,0,1:T(8,128)(2,1)}), bf16[128,8,512]{2,0,1:T(8,128)(2,1)S(1)}, u32[]{:S(2)}, u32[]{:S(2)}) async-start(bf16[128,8,512]{2,0,1:T(8,128)(2,1)} %bitcast.65), calls=%async_computation.1 | async-start | bytes 2097152 | tf_op jit(solution)/shard_map/all_to_all | solution.py:52
  49.8 375.9 %reduce-scatter.2.cloned.1.call-start = ((), (), s32[]{:S(2)}) async-start(), calls=%async_computation.6 | async-start | bytes 9437184 | tf_op jit(solution)/shard_map/reduce_scatter | solution.py:79
  228.0 5.6 %copy-start.6 = (bf16[512,4096]{1,0:T(8,128)(2,1)S(1)}, bf16[512,4096]{1,0:T(8,128)(2,1)}, u32[]{:S(2)}) copy-start(bf16[512,4096]{1,0:T(8,128)(2,1)} %param.13) | copy-start | bytes 12582916
  240.6 0.7 copy-start.4
  240.6 185.2 %copy-start.2 = (bf16[128,4096]{1,0:T(8,128)(2,1)S(1)}, bf16[128,4096]{1,0:T(8,128)(2,1)}, u32[]{:S(2)}) copy-start(bf16[128,4096]{1,0:T(8,128)(2,1)} %param.14) | copy-start | bytes 3145732
  241.3 189.2 %copy-start.1 = (bf16[128,1024]{1,0:T(8,128)(2,1)S(1)}, bf16[128,1024]{1,0:T(8,128)(2,1)}, u32[]{:S(2)}) copy-start(bf16[128,1024]{1,0:T(8,128)(2,1)} %param.9) | copy-start | bytes 786436
Sparse Core Ops, SparseCore 0:
  29.9 90.5 all-gather.2
  122.4 68.4 all-gather.4
  240.7 184.9 reduce-scatter.1
where the time goes:
time: 437 us
  waiting for transfers between devices  262 us (60%)
  local copies, waits for them, and re-layouts  90.7 us (21%)
  blocking collectives  34.7 us (8%)
  other arithmetic  15.9 us (4%)
  matrix products  15.6 us (4%)
  between operations  13.9 us (3%)
    reduce_scatter x1, waiting for transfers between devices, per_device(): lax.psum_scatter(partial_out, 'head', scatter_dimension=0, tiled=True)  184 us
    gather x1, local copies, waits for them, and re-layouts, attend_head(): key_sel = key_head[key_rows]  45.9 us
    gather x1, local copies, waits for them, and re-layouts, attend_head(): value_sel = value_head[key_rows]  37.2 us
    all_to_all x1, waiting for transfers between devices, per_device(): lax.all_to_all(rotated_query_rows, 'head', split_axis=1, concat_axis=0, t...  33.5 us
    all_gather x1, waiting for transfers between devices, per_device(): lax.all_gather(key_local, 'ctx', axis=0, tiled=True)  33.5 us
    all_to_all x1, blocking collectives, per_device(): lax.all_to_all(rotated_key_rows, 'head', split_axis=1, concat_axis=0, til...  21.6 us
    all_to_all x1, blocking collectives, per_device(): lax.all_to_all(value_row_matrix, 'head', split_axis=1, concat_axis=0, til...  13 us
    all_gather x1, waiting for transfers between devices, per_device(): lax.all_gather(value_local, 'ctx', axis=0, tiled=True)  11 us
  transfers between devices with their start and end apart: 4, of which 4 were waited for; matrix products, arithmetic and copies ran while one was open for 15% of the time, Pallas kernels for 0%

commit v1 on v0

v1 whole, which is shorter than its diff:
```python
import functools

import jax
import jax.numpy as jnp
from jax import lax
from jax.experimental import pallas as pl
from jax.experimental.pallas import tpu as pltpu
from jax.sharding import PartitionSpec as P

MESH = pl.DeviceIdType.MESH
HEAD_SIZE = 128
MASK_BLOCK_SIZE = 64
LANES = 128
GROUP = 4
NV = 8
NS = 4
RING = 4
HEADS = 8
CHUNKS = 4
D = 4096
CHUNK = D // CHUNKS
NEGATIVE = -1e30
EXPONENT_SCALE = HEAD_SIZE**-0.5 * 1.4426950408889634


def kernel(
    q_in, k_in, v_in, w_in, vert, slash, residual, gain,
    hidden_out, normed_out,
    kv, queries, weight, mixed, gathered, outgoing, incoming, stream,
    head_send, head_recv, query_send, query_recv, z_send, z_recv,
    right_send, right_recv, left_send, left_recv, core_send, core_recv,
    wright_send, wright_recv, wleft_send, wleft_recv, wcore_send, wcore_recv,
    mix_send, mix_recv, part_send, part_recv, local_sem,
):
    ctx = lax.axis_index("ctx")
    head = lax.axis_index("head")
    core, x, row = ctx % 2, (ctx // 2) % RING, ctx // (2 * RING)
    y, half = head % RING, head // RING

    def at_ctx(row_, x_, core_):
        return ((row_ * RING + x_) * 2 + core_, head)

    right = at_ctx(row, (x + 1) % RING, core)
    left = at_ctx(row, (x + 3) % RING, core)
    other_core = at_ctx(row, x, 1 - core)
    up = at_ctx((row + 1) % RING, x, core)
    down = at_ctx((row + 3) % RING, x, core)
    y_right = (ctx, half * RING + (y + 1) % RING)
    y_left = (ctx, half * RING + (y + 3) % RING)
    partner = (ctx, (1 - half) * RING + y)

    def head_peer(j):
        return (ctx, (head + j) % HEADS)

    def remote(src, dst, send, recv, device):
        return pltpu.make_async_remote_copy(
            src_ref=src, dst_ref=dst, send_sem=send, recv_sem=recv,
            device_id=device, device_id_type=MESH,
        )

    def landed(dst, recv):
        remote(dst, dst, recv, recv, other_core).wait_recv()

    def sent(src, send):
        remote(src, src, send, send, other_core).wait_send()

    barrier = pltpu.get_barrier_semaphore()
    friends = [head_peer(j) for j in range(1, HEADS)] + [right, left, other_core, up, down]
    for friend in friends:
        pl.semaphore_signal(barrier, inc=1, device_id=friend, device_id_type=MESH)

    def own_rows(n):
        return pltpu.make_async_copy(
            (k_in, v_in)[n].at[:, :, pl.ds(pl.multiple_of(head * LANES, LANES), LANES)],
            kv.at[n, pl.ds(ctx * 16 + head * 2, 2)],
            local_sem.at[n],
        )

    def own_queries():
        return pltpu.make_async_copy(
            q_in.at[:, pl.ds(pl.multiple_of(head * 512, 512), 512)],
            queries.at[head],
            local_sem.at[2],
        )

    def own_weight(n):
        return pltpu.make_async_copy(
            w_in.at[:, pl.ds(n * CHUNK, CHUNK)], weight.at[n, y], local_sem.at[3 + n]
        )

    own_rows(0).start()
    own_rows(1).start()
    pl.semaphore_wait(barrier, len(friends))

    def head_copy(j, n):
        peer = head_peer(j)
        src = (k_in, v_in)[n]
        return remote(
            src.at[:, :, pl.ds(pl.multiple_of(peer[1] * LANES, LANES), LANES)],
            kv.at[n, pl.ds(ctx * 16 + head * 2, 2)],
            head_send.at[n, j], head_recv.at[n, j], peer,
        )

    def query_copy(j):
        peer = head_peer(j)
        return remote(
            q_in.at[:, pl.ds(pl.multiple_of(peer[1] * 512, 512), 512)],
            queries.at[head],
            query_send.at[j], query_recv.at[j], peer,
        )

    for j in (4, 3, 5, 2, 6, 1, 7):
        for n in range(2):
            head_copy(j, n).start()
    for n in range(2):
        own_rows(n).wait()
    for j in range(1, HEADS):
        source = (head + HEADS - j) % HEADS
        for n in range(2):
            landed(kv.at[n, pl.ds(ctx * 16 + source * 2, 2)], head_recv.at[n, j])

    def piece(row_, x_, core_):
        return pl.ds(((row_ * RING + x_) * 2 + core_) * 16, 16)

    def half_rows(start, count):
        return pl.ds(pl.multiple_of(core * 256 + start, 128), count)

    def weight_first(n, direction):
        rows = half_rows(0, 256)
        src = w_in.at[rows, pl.ds(n * CHUNK, CHUNK)]
        dst = weight.at[n, y, rows]
        if direction > 0:
            return remote(src, dst, wright_send.at[n, 0], wright_recv.at[n, 0], y_right)
        return remote(src, dst, wleft_send.at[n, 0], wleft_recv.at[n, 0], y_left)

    def ctx_step(s):
        row_s = row - s
        own = kv.at[:, piece(row_s, x, core)]

        @pl.when(s > 0)
        def _():
            landed(own, z_recv.at[s])

        @pl.when(row < RING - 1)
        def _():
            remote(own, own, z_send.at[s], z_recv.at[s + 1], up).start()

        for n in (0, 1):
            part = kv.at[n, piece(row_s, x, core)]
            remote(part, part, right_send.at[s, n], right_recv.at[s, n], right).start()
            part = kv.at[1 - n, piece(row_s, x, core)]
            remote(part, part, left_send.at[s, 1 - n], left_recv.at[s, 1 - n], left).start()
        remote(own, own, core_send.at[s, 0], core_recv.at[s, 0], other_core).start()

        @pl.when(s > 0)
        def _():
            opposite(s - 1)

        @pl.when(s == 0)
        def _():
            for j in (4, 3, 5, 2, 6, 1, 7):
                query_copy(j).start()
            own_queries().start()
            for n in range(CHUNKS):
                own_weight(n).start()
                weight_first(n, 1).start()
                weight_first(n, -1).start()

        from_left = piece(row_s, (x + 3) % RING, core)
        from_right = piece(row_s, (x + 1) % RING, core)
        part = kv.at[0, from_left]
        landed(part, right_recv.at[s, 0])
        remote(part, part, right_send.at[s, 2], right_recv.at[s, 2], right).start()
        part = kv.at[1, from_right]
        landed(part, left_recv.at[s, 1])
        remote(part, part, left_send.at[s, 2], left_recv.at[s, 2], left).start()
        landed(kv.at[1, from_left], right_recv.at[s, 1])
        part = kv.at[:, from_left]
        remote(part, part, core_send.at[s, 1], core_recv.at[s, 1], other_core).start()
        landed(kv.at[0, from_right], left_recv.at[s, 0])
        part = kv.at[:, from_right]
        remote(part, part, core_send.at[s, 2], core_recv.at[s, 2], other_core).start()

    def opposite(s):
        far = piece(row - s, (x + 2) % RING, core)
        landed(kv.at[0, far], right_recv.at[s, 2])
        landed(kv.at[1, far], left_recv.at[s, 2])
        part = kv.at[:, far]
        remote(part, part, core_send.at[s, 3], core_recv.at[s, 3], other_core).start()

    def core_landed(s):
        for n, shift in enumerate((0, 3, 1, 2)):
            landed(kv.at[:, piece(row - s, (x + shift) % RING, 1 - core)], core_recv.at[s, n])

    def weight_step(n):
        from_left, from_right = (y + 3) % RING, (y + 1) % RING
        rows, low, high = half_rows(0, 256), half_rows(0, 128), half_rows(128, 128)
        landed(weight.at[n, from_left, rows], wright_recv.at[n, 0])
        part = weight.at[n, from_left, low]
        remote(part, part, wright_send.at[n, 1], wright_recv.at[n, 1], y_right).start()
        landed(weight.at[n, from_right, rows], wleft_recv.at[n, 0])
        part = weight.at[n, from_right, high]
        remote(part, part, wleft_send.at[n, 1], wleft_recv.at[n, 1], y_left).start()
        for m, source in enumerate((from_left, from_right)):
            part = weight.at[n, source, rows]
            remote(part, part, wcore_send.at[n, m], wcore_recv.at[n, m], other_core).start()

    def weight_far(n):
        far = (y + 2) % RING
        landed(weight.at[n, far, half_rows(0, 128)], wright_recv.at[n, 1])
        landed(weight.at[n, far, half_rows(128, 128)], wleft_recv.at[n, 1])
        part = weight.at[n, far, half_rows(0, 256)]
        remote(part, part, wcore_send.at[n, 2], wcore_recv.at[n, 2], other_core).start()

    def weight_landed(n):
        rows = pl.ds(pl.multiple_of((1 - core) * 256, 256), 256)
        for m, shift in enumerate((3, 1, 2)):
            landed(weight.at[n, (y + shift) % RING, rows], wcore_recv.at[n, m])

    lane = lax.broadcasted_iota(jnp.int32, (1, LANES), 1)
    diagonal_row = lax.broadcasted_iota(jnp.int32, (GROUP * MASK_BLOCK_SIZE, LANES), 0) % MASK_BLOCK_SIZE
    diagonal_lane = lax.broadcasted_iota(jnp.int32, (GROUP * MASK_BLOCK_SIZE, LANES), 1)
    future = (diagonal_lane < MASK_BLOCK_SIZE) & (diagonal_lane > diagonal_row)

    def attend(pair, b):
        block = pair * 2 + b
        blocks, biases = [], []
        for j in range(NV):
            entry = vert[0, j, block]
            blocks.append(jnp.maximum(entry, 0))
            biases.append(jnp.where(entry >= 0, 0.0, NEGATIVE).astype(jnp.float32))
        for j in range(NS):
            entry = slash[0, j, block]
            blocks.append(ctx * 16 + block - jnp.maximum(entry, 0))
            biases.append(jnp.where(entry >= 0, 0.0, NEGATIVE).astype(jnp.float32))
        rows = pl.ds(b * MASK_BLOCK_SIZE, MASK_BLOCK_SIZE)
        query = jnp.concatenate(
            [queries[pair, rows, pl.ds(g * HEAD_SIZE, HEAD_SIZE)] for g in range(GROUP)], axis=0
        )
        keys = jnp.concatenate([kv[0, n] for n in blocks], axis=0)
        scores = lax.dot_general(
            query, keys, (((1,), (1,)), ((), ())), preferred_element_type=jnp.float32
        )
        pieces = []
        for n in range((NV + NS) // 2):
            bias = jnp.where(lane < MASK_BLOCK_SIZE, biases[2 * n], biases[2 * n + 1])
            part = scores[:, n * LANES : (n + 1) * LANES] + bias
            if n == NV // 2:
                part = jnp.where(future, NEGATIVE, part)
            pieces.append(part)
        scores = jnp.concatenate(pieces, axis=1)
        top = jnp.max(scores, axis=-1, keepdims=True)
        weights = jnp.exp2((scores - top) * EXPONENT_SCALE)
        total = jnp.sum(weights, axis=-1, keepdims=True)
        values = jnp.concatenate([kv[1, n] for n in blocks], axis=0)
        out = jnp.dot(weights.astype(jnp.bfloat16), values, preferred_element_type=jnp.float32)
        out = (out / total).astype(jnp.bfloat16)
        for g in range(GROUP):
            mixed[pair, rows, pl.ds(g * HEAD_SIZE, HEAD_SIZE)] = out[
                g * MASK_BLOCK_SIZE : (g + 1) * MASK_BLOCK_SIZE
            ]

    def mix_place(m):
        turn, j = m // RING, m % RING + 1
        token_half = (1 - half) * (1 - turn) + half * turn
        return turn, j, token_half, (y + j) % RING

    def attention():
        lax.fori_loop(0, row + 1, lambda s, carry: (core_landed(s), carry)[1], 0)
        own_queries().wait()
        for j in range(1, HEADS):
            landed(queries.at[(head + HEADS - j) % HEADS], query_recv.at[j])

        def pair_step(m, carry):
            turn, j, token_half, target = mix_place(m)
            pair = token_half * RING + target
            for b in range(2):
                attend(pair, b)

            @pl.when(j < RING)
            def _():
                remote(
                    mixed.at[pair], gathered.at[token_half, y],
                    mix_send.at[m], mix_recv.at[m], (ctx, half * RING + target),
                ).start()

            @pl.when(j == RING)
            def _():
                gathered[token_half, y] = mixed[pair]

            return carry

        lax.fori_loop(0, 2 * RING, pair_step, 0)

    def mix_landed(turn):
        token_half = 1 - half if turn == 0 else half
        for j in range(1, RING):
            landed(gathered.at[token_half, (y + RING - j) % RING], mix_recv.at[turn * RING + j - 1])

    def project(token_half, n, columns):
        total = None
        for source in range(RING):
            term = jnp.dot(
                gathered[token_half, source], weight[n, source, :, columns],
                preferred_element_type=jnp.float32,
            )
            total = term if total is None else total + term
        return total

    def send_part(n, carry):
        weight_landed(n)
        for t in range(CHUNK // 512):
            columns = pl.ds(t * 512, 512)
            outgoing[n, :, columns] = project(1 - half, n, columns).astype(jnp.bfloat16)
        remote(
            outgoing.at[n], incoming.at[n], part_send.at[n], part_recv.at[n], partner
        ).start()
        return carry

    def step(s, carry):
        @pl.when(s <= row)
        def _():
            ctx_step(s)

        @pl.when(s < CHUNKS)
        def _():
            weight_step(s)

        @pl.when(s == row)
        def _():
            opposite(s)
            attention()

        @pl.when(s > 0)
        def _():
            weight_far(s - 1)

        @pl.when(s == row + 1)
        def _():
            for n in range(CHUNKS):
                own_weight(n).wait()
            mix_landed(0)

        first = jnp.where(s == row + 1, 0, s - 1)
        last = jnp.where(s > row, s, first)
        lax.fori_loop(first, last, send_part, 0)
        return carry

    lax.fori_loop(0, CHUNKS + 1, step, 0)

    mix_landed(1)

    def own_part(n, carry):
        for t in range(CHUNK // 512):
            columns = pl.ds(t * 512, 512)
            stream[n, :, columns] = project(half, n, columns)
        return carry

    lax.fori_loop(0, CHUNKS, own_part, 0)

    square = jnp.zeros((128, 1), jnp.float32)
    for n in range(CHUNKS):
        landed(incoming.at[n], part_recv.at[n])
        columns = slice(n * CHUNK, (n + 1) * CHUNK)
        value = (
            residual[:, columns].astype(jnp.float32)
            + stream[n]
            + incoming[n].astype(jnp.float32)
        )
        stream[n] = value
        hidden_out[:, columns] = value.astype(jnp.bfloat16)
        square = square + jnp.sum(value * value, axis=-1, keepdims=True)
    scale = lax.rsqrt(square * (1.0 / D) + 1e-05)
    for n in range(D // LANES):
        place = n * LANES % CHUNK
        value = stream[n * LANES // CHUNK, :, place : place + LANES]
        normed_out[:, n * LANES : (n + 1) * LANES] = (
            value * scale * gain[n : n + 1].astype(jnp.float32)
        ).astype(jnp.bfloat16)

    for j in range(1, HEADS):
        for n in range(2):
            head_copy(j, n).wait_send()
        query_copy(j).wait_send()

    def ctx_sent(s, carry):
        own = kv.at[:, piece(row - s, x, core)]

        @pl.when(row < RING - 1)
        def _():
            sent(own, z_send.at[s])

        for n in range(3):
            part = kv.at[0, piece(row - s, x, core)]
            sent(part, right_send.at[s, n])
            sent(part, left_send.at[s, n])
        for n in range(4):
            sent(own, core_send.at[s, n])
        return carry

    lax.fori_loop(0, row + 1, ctx_sent, 0)

    def weight_sent(n, carry):
        rows, low = half_rows(0, 256), half_rows(0, 128)
        sent(weight.at[n, y, rows], wright_send.at[n, 0])
        sent(weight.at[n, y, rows], wleft_send.at[n, 0])
        sent(weight.at[n, y, low], wright_send.at[n, 1])
        sent(weight.at[n, y, low], wleft_send.at[n, 1])
        for m in range(3):
            sent(weight.at[n, y, rows], wcore_send.at[n, m])
        sent(outgoing.at[n], part_send.at[n])
        return carry

    lax.fori_loop(0, CHUNKS, weight_sent, 0)
    for turn in range(2):
        for j in range(1, RING):
            sent(mixed.at[0], mix_send.at[turn * RING + j - 1])


def per_device(q, k, v, vert, slash, out_weight, residual, norm_gain):
    anywhere = pl.BlockSpec(memory_space=pl.ANY)
    vmem = pl.BlockSpec(memory_space=pltpu.VMEM)
    smem = pl.BlockSpec(memory_space=pltpu.SMEM)
    dma = pltpu.SemaphoreType.DMA
    tokens = q.shape[0]
    return pl.pallas_call(
        kernel,
        out_shape=[jax.ShapeDtypeStruct((tokens, D), jnp.bfloat16)] * 2,
        in_specs=[anywhere] * 4 + [smem, smem, vmem, vmem],
        out_specs=[vmem, vmem],
        scratch_shapes=[
            pltpu.VMEM((2, 512, MASK_BLOCK_SIZE, HEAD_SIZE), jnp.bfloat16),
            pltpu.VMEM((HEADS, tokens, 512), jnp.bfloat16),
            pltpu.VMEM((CHUNKS, RING, 512, CHUNK), jnp.bfloat16),
            pltpu.VMEM((HEADS, tokens, 512), jnp.bfloat16),
            pltpu.VMEM((2, RING, tokens, 512), jnp.bfloat16),
            pltpu.VMEM((CHUNKS, tokens, CHUNK), jnp.bfloat16),
            pltpu.VMEM((CHUNKS, tokens, CHUNK), jnp.bfloat16),
            pltpu.VMEM((CHUNKS, tokens, CHUNK), jnp.float32),
            dma((2, HEADS)), dma((2, HEADS)), dma((HEADS,)), dma((HEADS,)),
            dma((RING,)), dma((RING,)),
            dma((RING, 3)), dma((RING, 3)), dma((RING, 3)), dma((RING, 3)),
            dma((RING, 4)), dma((RING, 4)),
            dma((CHUNKS, 2)), dma((CHUNKS, 2)), dma((CHUNKS, 2)), dma((CHUNKS, 2)),
            dma((CHUNKS, 3)), dma((CHUNKS, 3)),
            dma((2 * RING,)), dma((2 * RING,)), dma((CHUNKS,)), dma((CHUNKS,)),
            dma((3 + CHUNKS,)),
        ],
        compiler_params=pltpu.CompilerParams(
            collective_id=0, has_side_effects=True, vmem_limit_bytes=58 * 1024 * 1024
        ),
        cost_estimate=pl.CostEstimate(
            flops=6_000_000_000, bytes_accessed=10_000_000, transcendentals=3_200_000
        ),
        name="attention_layer",
    )(
        q,
        k.reshape(tokens // MASK_BLOCK_SIZE, MASK_BLOCK_SIZE, -1),
        v.reshape(tokens // MASK_BLOCK_SIZE, MASK_BLOCK_SIZE, -1),
        out_weight, vert.transpose(0, 2, 1), slash.transpose(0, 2, 1), residual,
        norm_gain.reshape(D // LANES, LANES),
    )


def solution(mesh):
    token_rows = P(("ctx", "head"), None)
    return jax.shard_map(
        lambda *args: tuple(per_device(*args)),
        mesh=mesh,
        in_specs=(
            token_rows, token_rows, token_rows,
            P("head", "ctx", None), P("head", "ctx", None),
            P("head", None), token_rows, P(),
        ),
        out_specs=(token_rows, token_rows),
        check_vma=False,
    )
```

time: 437 us -> 170 us (0.39)
  the two profiles are of different devices: /device:TPU:1 before, /device:TPU:225 now
where the time goes in v1:
time: 170 us
  Pallas kernels  164 us (96%)
  local copies, waits for them, and re-layouts  4.57 us (3%)
    pallas_call x1, Pallas kernels, per_device(): pl.pallas_call(kernel, out_shape=[jax.ShapeDtypeStruct((tokens, D), jnp.b...  164 us
    unnamed x2, local copies, waits for them, and re-layouts  4.57 us

profile of v1, /device:TPU:225, one launch (start us, length us, event | category | flops | bytes accessed | tf_op | source)
XLA Modules:
  0.0 169.6 jit_solution(4309351490534275215)
XLA Ops:
  0.6 164.4 %attention_layer.1 = (bf16[128,4096]{1,0:T(8,128)(2,1)}, bf16[128,4096]{1,0:T(8,128)(2,1)}) custom-call(bf16[128,4096]{1,0:T(8,128)(2,1)} %q_in.1, bf16[2,64,1024]{2,1,0:T(8,128)(2,1)} %bitcast.5, bf16[2,64,1024]{2,1,0:T(8,128)(2,1)} %bitcast.6, bf16[512,4096]{1,0:T(8,128)(2,1)} %w_in.1, s32[1,8,16]{2,1,0:T(8,128)} %bitcast.8, s32[1,4,16]{2,1,0:T(4,128)} %bitcast.9, ...), custom_call_target="tpu_custom_call" | custom-call | flops 6000000000 | bytes 10000000 | tf_op jit(solution)/shard_map/attention_layer/pallas_call | solution.py:426
  165.1 2.3 %copy.12 = bf16[128,4096]{1,0:T(8,128)(2,1)} copy(bf16[128,4096]{1,0:T(8,128)(2,1)} %get-tuple-element.4) | data formatting | bytes 2097152
  167.4 2.3 %copy.13 = bf16[128,4096]{1,0:T(8,128)(2,1)} copy(bf16[128,4096]{1,0:T(8,128)(2,1)} %get-tuple-element.5) | data formatting | bytes 2097152

commit v2 on v1

--- a/solution.py
+++ b/solution.py
@@ -24,10 +24,11 @@
 
 
 def kernel(
-    q_in, k_in, v_in, w_in, vert, slash, residual, gain,
-    hidden_out, normed_out,
-    kv, queries, weight, mixed, gathered, outgoing, incoming, stream,
-    head_send, head_recv, query_send, query_recv, z_send, z_recv,
+    q_in, k_in, v_in, w_in, vert, slash,
+    stream,
+    kv, queries, weight, mixed, gathered, outgoing, incoming,
+    near_send, near_recv, far_send, far_recv, query_send, query_recv,
+    up_send, up_recv, down_send, down_recv,
     right_send, right_recv, left_send, left_recv, core_send, core_recv,
     wright_send, wright_recv, wleft_send, wleft_recv, wcore_send, wcore_recv,
     mix_send, mix_recv, part_send, part_recv, local_sem,
@@ -64,10 +65,21 @@
     def sent(src, send):
         remote(src, src, send, send, other_core).wait_send()
 
+    def far_peer(row_, y_):
+        return ((row_ * RING + x) * 2 + core, (1 - half) * RING + y_)
+
     barrier = pltpu.get_barrier_semaphore()
     friends = [head_peer(j) for j in range(1, HEADS)] + [right, left, other_core, up, down]
     for friend in friends:
         pl.semaphore_signal(barrier, inc=1, device_id=friend, device_id_type=MESH)
+
+    @pl.when(row == RING - 1)
+    def _():
+        for row_ in range(RING - 1):
+            for y_ in range(RING):
+                pl.semaphore_signal(
+                    barrier, inc=1, device_id=far_peer(row_, y_), device_id_type=MESH
+                )
 
     def own_rows(n):
         return pltpu.make_async_copy(
@@ -90,15 +102,24 @@
 
     own_rows(0).start()
     own_rows(1).start()
-    pl.semaphore_wait(barrier, len(friends))
-
-    def head_copy(j, n):
-        peer = head_peer(j)
+    pl.semaphore_wait(barrier, len(friends) + jnp.where(row < RING - 1, RING, 0))
+
+    def key_value_copy(n, target, send, recv, device):
         src = (k_in, v_in)[n]
         return remote(
-            src.at[:, :, pl.ds(pl.multiple_of(peer[1] * LANES, LANES), LANES)],
-            kv.at[n, pl.ds(ctx * 16 + head * 2, 2)],
-            head_send.at[n, j], head_recv.at[n, j], peer,
+            src.at[:, :, pl.ds(pl.multiple_of(target * LANES, LANES), LANES)],
+            kv.at[n, pl.ds(ctx * 16 + head * 2, 2)], send, recv, device,
+        )
+
+    def near_copy(j, n):
+        target = half * RING + (y + j) % RING
+        return key_value_copy(n, target, near_send.at[j, n], near_recv.at[j, n], (ctx, target))
+
+    def far_copy(j, n):
+        y_ = (y + j) % RING
+        device = far_peer(RING - 1, y_)
+        return key_value_copy(
+            n, device[1], far_send.at[j, n], far_recv.at[row, j, n], device
         )
 
     def query_copy(j):
@@ -109,88 +130,116 @@
             query_send.at[j], query_recv.at[j], peer,
         )
 
-    for j in (4, 3, 5, 2, 6, 1, 7):
+    for j in (1, 3, 2):
         for n in range(2):
-            head_copy(j, n).start()
-    for n in range(2):
-        own_rows(n).wait()
-    for j in range(1, HEADS):
-        source = (head + HEADS - j) % HEADS
+            near_copy(j, n).start()
+    for j in range(RING):
         for n in range(2):
-            landed(kv.at[n, pl.ds(ctx * 16 + source * 2, 2)], head_recv.at[n, j])
-
-    def piece(row_, x_, core_):
-        return pl.ds(((row_ * RING + x_) * 2 + core_) * 16, 16)
+            far_copy(j, n).start()
+
+    def piece(row_, x_, core_, u):
+        owner = half if u == 0 else 1 - half
+        return pl.ds(((row_ * RING + x_) * 2 + core_) * 16 + owner * 8, 8)
+
+    def far_landed(row_):
+        @pl.when(row == RING - 1)
+        def _():
+            for j in range(RING):
+                source = (1 - half) * RING + (y + RING - j) % RING
+                place = pl.ds(((row_ * RING + x) * 2 + core) * 16 + source * 2, 2)
+                for n in range(2):
+                    landed(kv.at[n, place], far_recv.at[row_, j, n])
+
+        @pl.when(row < RING - 1)
+        def _():
+            landed(kv.at[:, piece(row_, x, core, 1)], down_recv.at[row_])
+
+    def hand_down(row_, carry):
+        far_landed(row_)
+        part = kv.at[:, piece(row_, x, core, 1)]
+        remote(part, part, down_send.at[row_], down_recv.at[row_], down).start()
+        return carry
 
     def half_rows(start, count):
         return pl.ds(pl.multiple_of(core * 256 + start, 128), count)
 
-    def weight_first(n, direction):
+    def weight_first(n):
         rows = half_rows(0, 256)
         src = w_in.at[rows, pl.ds(n * CHUNK, CHUNK)]
         dst = weight.at[n, y, rows]
-        if direction > 0:
-            return remote(src, dst, wright_send.at[n, 0], wright_recv.at[n, 0], y_right)
-        return remote(src, dst, wleft_send.at[n, 0], wleft_recv.at[n, 0], y_left)
-
-    def ctx_step(s):
+        remote(src, dst, wright_send.at[n, 0], wright_recv.at[n, 0], y_right).start()
+        remote(src, dst, wleft_send.at[n, 0], wleft_recv.at[n, 0], y_left).start()
+
+    for n in range(CHUNKS):
+        weight_first(n)
+
+    def ctx_step(s, u):
         row_s = row - s
-        own = kv.at[:, piece(row_s, x, core)]
+        q = u * RING + s
+        own = kv.at[:, piece(row_s, x, core, u)]
+        if u == 0:
+            @pl.when(s == 0)
+            def _():
+                for n in range(2):
+                    own_rows(n).wait()
+                for j in range(1, RING):
+                    source = half * RING + (y + RING - j) % RING
+                    for n in range(2):
+                        landed(kv.at[n, pl.ds(ctx * 16 + source * 2, 2)], near_recv.at[j, n])
+
+            @pl.when(s > 0)
+            def _():
+                landed(own, up_recv.at[s])
+
+            @pl.when(row < RING - 1)
+            def _():
+                remote(own, own, up_send.at[s], up_recv.at[s + 1], up).start()
+        else:
+            @pl.when(s == 0)
+            def _():
+                far_landed(row)
+
+        for n in (0, 1):
+            part = kv.at[n, piece(row_s, x, core, u)]
+            remote(part, part, right_send.at[q, n], right_recv.at[q, n], right).start()
+            part = kv.at[1 - n, piece(row_s, x, core, u)]
+            remote(part, part, left_send.at[q, 1 - n], left_recv.at[q, 1 - n], left).start()
+        remote(own, own, core_send.at[q, 0], core_recv.at[q, 0], other_core).start()
 
         @pl.when(s > 0)
         def _():
-            landed(own, z_recv.at[s])
-
-        @pl.when(row < RING - 1)
-        def _():
-            remote(own, own, z_send.at[s], z_recv.at[s + 1], up).start()
-
-        for n in (0, 1):
-            part = kv.at[n, piece(row_s, x, core)]
-            remote(part, part, right_send.at[s, n], right_recv.at[s, n], right).start()
-            part = kv.at[1 - n, piece(row_s, x, core)]
-            remote(part, part, left_send.at[s, 1 - n], left_recv.at[s, 1 - n], left).start()
-        remote(own, own, core_send.at[s, 0], core_recv.at[s, 0], other_core).start()
-
-        @pl.when(s > 0)
-        def _():
-            opposite(s - 1)
-
-        @pl.when(s == 0)
-        def _():
-            for j in (4, 3, 5, 2, 6, 1, 7):
-                query_copy(j).start()
-            own_queries().start()
-            for n in range(CHUNKS):
-                own_weight(n).start()
-                weight_first(n, 1).start()
-                weight_first(n, -1).start()
-
-        from_left = piece(row_s, (x + 3) % RING, core)
-        from_right = piece(row_s, (x + 1) % RING, core)
+            opposite(s - 1, u)
+
+        from_left = piece(row_s, (x + 3) % RING, core, u)
+        from_right = piece(row_s, (x + 1) % RING, core, u)
         part = kv.at[0, from_left]
-        landed(part, right_recv.at[s, 0])
-        remote(part, part, right_send.at[s, 2], right_recv.at[s, 2], right).start()
+        landed(part, right_recv.at[q, 0])
+        remote(part, part, right_send.at[q, 2], right_recv.at[q, 2], right).start()
         part = kv.at[1, from_right]
-        landed(part, left_recv.at[s, 1])
-        remote(part, part, left_send.at[s, 2], left_recv.at[s, 2], left).start()
-        landed(kv.at[1, from_left], right_recv.at[s, 1])
+        landed(part, left_recv.at[q, 1])
+        remote(part, part, left_send.at[q, 2], left_recv.at[q, 2], left).start()
+        landed(kv.at[1, from_left], right_recv.at[q, 1])
         part = kv.at[:, from_left]
-        remote(part, part, core_send.at[s, 1], core_recv.at[s, 1], other_core).start()
-        landed(kv.at[0, from_right], left_recv.at[s, 0])
+        remote(part, part, core_send.at[q, 1], core_recv.at[q, 1], other_core).start()
+        landed(kv.at[0, from_right], left_recv.at[q, 0])
         part = kv.at[:, from_right]
-        remote(part, part, core_send.at[s, 2], core_recv.at[s, 2], other_core).start()
-
-    def opposite(s):
-        far = piece(row - s, (x + 2) % RING, core)
-        landed(kv.at[0, far], right_recv.at[s, 2])
-        landed(kv.at[1, far], left_recv.at[s, 2])
+        remote(part, part, core_send.at[q, 2], core_recv.at[q, 2], other_core).start()
+
+    def opposite(s, u):
+        far, q = piece(row - s, (x + 2) % RING, core, u), u * RING + s
+        landed(kv.at[0, far], right_recv.at[q, 2])
+        landed(kv.at[1, far], left_recv.at[q, 2])
         part = kv.at[:, far]
-        remote(part, part, core_send.at[s, 3], core_recv.at[s, 3], other_core).start()
-
-    def core_landed(s):
-        for n, shift in enumerate((0, 3, 1, 2)):
-            landed(kv.at[:, piece(row - s, (x + shift) % RING, 1 - core)], core_recv.at[s, n])
+        remote(part, part, core_send.at[q, 3], core_recv.at[q, 3], other_core).start()
+
+    def core_landed(s, carry):
+        for u in range(2):
+            for n, shift in enumerate((0, 3, 1, 2)):
+                landed(
+                    kv.at[:, piece(row - s, (x + shift) % RING, 1 - core, u)],
+                    core_recv.at[u * RING + s, n],
+                )
+        return carry
 
     def weight_step(n):
         from_left, from_right = (y + 3) % RING, (y + 1) % RING
@@ -265,12 +314,13 @@
         token_half = (1 - half) * (1 - turn) + half * turn
         return turn, j, token_half, (y + j) % RING
 
-    def attention():
-        lax.fori_loop(0, row + 1, lambda s, carry: (core_landed(s), carry)[1], 0)
+    def operands_landed():
+        lax.fori_loop(0, row + 1, core_landed, 0)
         own_queries().wait()
         for j in range(1, HEADS):
             landed(queries.at[(head + HEADS - j) % HEADS], query_recv.at[j])
 
+    def attention(first, last):
         def pair_step(m, carry):
             turn, j, token_half, target = mix_place(m)
             pair = token_half * RING + target
@@ -290,7 +340,7 @@
 
             return carry
 
-        lax.fori_loop(0, 2 * RING, pair_step, 0)
+        lax.fori_loop(first, last, pair_step, 0)
 
     def mix_landed(turn):
         token_half = 1 - half if turn == 0 else half
@@ -317,23 +367,41 @@
         ).start()
         return carry
 
+    last_row = row == RING - 1
+
+    def first_half(s, carry):
+        ctx_step(s, 0)
+        first = jnp.where(last_row, jnp.maximum(s - 1, 0), 0)
+        last = jnp.where(last_row | (s == row), s, 0)
+        lax.fori_loop(first, last, hand_down, 0)
+        return carry
+
+    for j in (4, 3, 5, 2, 6, 1, 7):
+        query_copy(j).start()
+    lax.fori_loop(0, row + 1, first_half, 0)
+    own_queries().start()
+    for n in range(CHUNKS):
+        own_weight(n).start()
+    opposite(row, 0)
+
     def step(s, carry):
         @pl.when(s <= row)
         def _():
-            ctx_step(s)
+            ctx_step(s, 1)
 
         @pl.when(s < CHUNKS)
         def _():
             weight_step(s)
 
+        @pl.when(s > 0)
+        def _():
+            weight_far(s - 1)
+
         @pl.when(s == row)
         def _():
-            opposite(s)
-            attention()
-
-        @pl.when(s > 0)
-        def _():
-            weight_far(s - 1)
+            opposite(s, 1)
+            operands_landed()
+            attention(0, RING)
 
         @pl.when(s == row + 1)
         def _():
@@ -348,6 +416,7 @@
 
     lax.fori_loop(0, CHUNKS + 1, step, 0)
 
+    attention(RING, 2 * RING)
     mix_landed(1)
 
     def own_part(n, carry):
@@ -358,44 +427,38 @@
 
     lax.fori_loop(0, CHUNKS, own_part, 0)
 
-    square = jnp.zeros((128, 1), jnp.float32)
     for n in range(CHUNKS):
         landed(incoming.at[n], part_recv.at[n])
-        columns = slice(n * CHUNK, (n + 1) * CHUNK)
-        value = (
-            residual[:, columns].astype(jnp.float32)
-            + stream[n]
-            + incoming[n].astype(jnp.float32)
-        )
-        stream[n] = value
-        hidden_out[:, columns] = value.astype(jnp.bfloat16)
-        square = square + jnp.sum(value * value, axis=-1, keepdims=True)
-    scale = lax.rsqrt(square * (1.0 / D) + 1e-05)
-    for n in range(D // LANES):
-        place = n * LANES % CHUNK
-        value = stream[n * LANES // CHUNK, :, place : place + LANES]
-        normed_out[:, n * LANES : (n + 1) * LANES] = (
-            value * scale * gain[n : n + 1].astype(jnp.float32)
-        ).astype(jnp.bfloat16)
+        stream[n] = stream[n] + incoming[n].astype(jnp.float32)
 
     for j in range(1, HEADS):
-        for n in range(2):
-            head_copy(j, n).wait_send()
         query_copy(j).wait_send()
+    for n in range(2):
+        for j in range(RING):
+            if j > 0:
+                near_copy(j, n).wait_send()
+            far_copy(j, n).wait_send()
+
+    def down_sent(row_, carry):
+        sent(kv.at[:, piece(row_, x, core, 1)], down_send.at[row_])
+        return carry
+
+    lax.fori_loop(0, row, down_sent, 0)
 
     def ctx_sent(s, carry):
-        own = kv.at[:, piece(row - s, x, core)]
+        own = kv.at[:, piece(row - s, x, core, 0)]
+        part = kv.at[0, piece(row - s, x, core, 0)]
 
         @pl.when(row < RING - 1)
         def _():
-            sent(own, z_send.at[s])
-
-        for n in range(3):
-            part = kv.at[0, piece(row - s, x, core)]
-            sent(part, right_send.at[s, n])
-            sent(part, left_send.at[s, n])
-        for n in range(4):
-            sent(own, core_send.at[s, n])
+            sent(own, up_send.at[s])
+
+        for u in range(2):
+            for n in range(3):
+                sent(part, right_send.at[u * RING + s, n])
+                sent(part, left_send.at[u * RING + s, n])
+            for n in range(4):
+                sent(own, core_send.at[u * RING + s, n])
         return carry
 
     lax.fori_loop(0, row + 1, ctx_sent, 0)
@@ -417,17 +480,35 @@
             sent(mixed.at[0], mix_send.at[turn * RING + j - 1])
 
 
+def finish(stream, residual, gain, hidden_out, normed_out):
+    square = jnp.zeros((stream.shape[1], 1), jnp.float32)
+    values = []
+    for n in range(CHUNKS):
+        columns = slice(n * CHUNK, (n + 1) * CHUNK)
+        value = stream[n] + residual[:, columns].astype(jnp.float32)
+        hidden_out[:, columns] = value.astype(jnp.bfloat16)
+        square = square + jnp.sum(value * value, axis=-1, keepdims=True)
+        values.append(value)
+    scale = lax.rsqrt(square * (1.0 / D) + 1e-05)
+    for n in range(D // LANES):
+        place = n * LANES % CHUNK
+        value = values[n * LANES // CHUNK][:, place : place + LANES]
+        normed_out[:, n * LANES : (n + 1) * LANES] = (
+            value * scale * gain[n : n + 1].astype(jnp.float32)
+        ).astype(jnp.bfloat16)
+
+
 def per_device(q, k, v, vert, slash, out_weight, residual, norm_gain):
     anywhere = pl.BlockSpec(memory_space=pl.ANY)
     vmem = pl.BlockSpec(memory_space=pltpu.VMEM)
     smem = pl.BlockSpec(memory_space=pltpu.SMEM)
     dma = pltpu.SemaphoreType.DMA
     tokens = q.shape[0]
-    return pl.pallas_call(
+    stream = pl.pallas_call(
         kernel,
-        out_shape=[jax.ShapeDtypeStruct((tokens, D), jnp.bfloat16)] * 2,
-        in_specs=[anywhere] * 4 + [smem, smem, vmem, vmem],
-        out_specs=[vmem, vmem],
+        out_shape=jax.ShapeDtypeStruct((CHUNKS, tokens, CHUNK), jnp.float32),
+        in_specs=[anywhere] * 4 + [smem, smem],
+        out_specs=vmem,
         scratch_shapes=[
             pltpu.VMEM((2, 512, MASK_BLOCK_SIZE, HEAD_SIZE), jnp.bfloat16),
             pltpu.VMEM((HEADS, tokens, 512), jnp.bfloat16),
@@ -436,18 +517,18 @@
             pltpu.VMEM((2, RING, tokens, 512), jnp.bfloat16),
             pltpu.VMEM((CHUNKS, tokens, CHUNK), jnp.bfloat16),
             pltpu.VMEM((CHUNKS, tokens, CHUNK), jnp.bfloat16),
-            pltpu.VMEM((CHUNKS, tokens, CHUNK), jnp.float32),
-            dma((2, HEADS)), dma((2, HEADS)), dma((HEADS,)), dma((HEADS,)),
-            dma((RING,)), dma((RING,)),
-            dma((RING, 3)), dma((RING, 3)), dma((RING, 3)), dma((RING, 3)),
-            dma((RING, 4)), dma((RING, 4)),
+            dma((RING, 2)), dma((RING, 2)), dma((RING, 2)), dma((RING, RING, 2)),
+            dma((HEADS,)), dma((HEADS,)),
+            dma((RING,)), dma((RING,)), dma((RING,)), dma((RING,)),
+            dma((2 * RING, 3)), dma((2 * RING, 3)), dma((2 * RING, 3)), dma((2 * RING, 3)),
+            dma((2 * RING, 4)), dma((2 * RING, 4)),
             dma((CHUNKS, 2)), dma((CHUNKS, 2)), dma((CHUNKS, 2)), dma((CHUNKS, 2)),
             dma((CHUNKS, 3)), dma((CHUNKS, 3)),
             dma((2 * RING,)), dma((2 * RING,)), dma((CHUNKS,)), dma((CHUNKS,)),
             dma((3 + CHUNKS,)),
         ],
         compiler_params=pltpu.CompilerParams(
-            collective_id=0, has_side_effects=True, vmem_limit_bytes=58 * 1024 * 1024
+            collective_id=0, has_side_effects=True, vmem_limit_bytes=54 * 1024 * 1024
         ),
         cost_estimate=pl.CostEstimate(
             flops=6_000_000_000, bytes_accessed=10_000_000, transcendentals=3_200_000
@@ -457,9 +538,22 @@
         q,
         k.reshape(tokens // MASK_BLOCK_SIZE, MASK_BLOCK_SIZE, -1),
         v.reshape(tokens // MASK_BLOCK_SIZE, MASK_BLOCK_SIZE, -1),
-        out_weight, vert.transpose(0, 2, 1), slash.transpose(0, 2, 1), residual,
-        norm_gain.reshape(D // LANES, LANES),
+        out_weight, vert.transpose(0, 2, 1), slash.transpose(0, 2, 1),
     )
+    rows = 32
+    row_block = pl.BlockSpec((rows, D), lambda i: (i, 0))
+    return pl.pallas_call(
+        finish,
+        grid=(tokens // rows,),
+        out_shape=[jax.ShapeDtypeStruct((tokens, D), jnp.bfloat16)] * 2,
+        in_specs=[
+            pl.BlockSpec((CHUNKS, rows, CHUNK), lambda i: (0, i, 0)),
+            row_block,
+            pl.BlockSpec((D // LANES, LANES), lambda i: (0, 0)),
+        ],
+        out_specs=[row_block, row_block],
+        name="residual_norm",
+    )(stream, residual, norm_gain.reshape(D // LANES, LANES))
 
 
 def solution(mesh):

time: 170 us -> 164 us (0.965); the launches traced: 170 us -> 161 us
  local copies, waits for them, and re-layouts: 4.57 us -> 0 us
  Pallas kernels: 164 us -> 161 us
    unnamed x2 -> x0, local copies, waits for them, and re-layouts: 4.57 us -> none
    pallas_call x1 -> x2, Pallas kernels: 164 us -> 161 us  [the longest x1 157 us: per_device(): pl.pallas_call(kernel, out_shape=jax.ShapeDtypeStruct((CHUNKS, tokens, CH...]
where the time goes in v2:
time: 164 us; the launch traced here: 161 us
  Pallas kernels  161 us (98%)
    pallas_call x1, Pallas kernels, per_device(): pl.pallas_call(kernel, out_shape=jax.ShapeDtypeStruct((CHUNKS, tokens, CH...  157 us
    pallas_call x1, Pallas kernels, per_device(): pl.pallas_call(finish, grid=(tokens // rows,), out_shape=[jax.ShapeDtypeS...  4.16 us

profile of v2, /device:TPU:225, one launch (start us, length us, event | category | flops | bytes accessed | tf_op | source)
XLA Modules:
  0.0 161.5 jit_solution(14274583465481706659)
XLA Ops:
  0.6 156.7 %attention_layer.1.stream = f32[4,128,1024]{2,1,0:T(8,128)} custom-call(bf16[128,4096]{1,0:T(8,128)(2,1)} %q_in.1, bf16[2,64,1024]{2,1,0:T(8,128)(2,1)} %bitcast.6, bf16[2,64,1024]{2,1,0:T(8,128)(2,1)} %bitcast.7, bf16[512,4096]{1,0:T(8,128)(2,1)} %w_in.1, s32[1,8,16]{2,1,0:T(8,128)} %bitcast.8, s32[1,4,16]{2,1,0:T(4,128)} %bitcast.9), custom_call_target="tpu_custom_call" | custom-call | flops 6000000000 | bytes 10000000 | tf_op jit(solution)/shard_map/attention_layer/pallas_call | solution.py:507
  157.3 4.2 %residual_norm.1 = (bf16[128,4096]{1,0:T(8,128)(2,1)}, bf16[128,4096]{1,0:T(8,128)(2,1)}) custom-call(f32[4,128,1024]{2,1,0:T(8,128)} %attention_layer.1.stream, bf16[128,4096]{1,0:T(8,128)(2,1)} %residual.1, bf16[32,128]{1,0:T(8,128)(2,1)} %bitcast.5), custom_call_target="tpu_custom_call" | custom-call | tf_op jit(solution)/shard_map/residual_norm/pallas_call | solution.py:545

commit v3 on v2

--- a/solution.py
+++ b/solution.py
@@ -200,10 +200,16 @@
                 far_landed(row)
 
         for n in (0, 1):
-            part = kv.at[n, piece(row_s, x, core, u)]
-            remote(part, part, right_send.at[q, n], right_recv.at[q, n], right).start()
-            part = kv.at[1 - n, piece(row_s, x, core, u)]
-            remote(part, part, left_send.at[q, 1 - n], left_recv.at[q, 1 - n], left).start()
+            def to_right(n=n):
+                part = kv.at[n, piece(row_s, x, core, u)]
+                remote(part, part, right_send.at[q, n], right_recv.at[q, n], right).start()
+
+            def to_left(n=n):
+                part = kv.at[1 - n, piece(row_s, x, core, u)]
+                remote(part, part, left_send.at[q, 1 - n], left_recv.at[q, 1 - n], left).start()
+
+            pl.when((s > 0) | (x < 3))(to_right)
+            pl.when((s > 0) | (x == 0) | ((x == 1) & (n == 0)))(to_left)
         remote(own, own, core_send.at[q, 0], core_recv.at[q, 0], other_core).start()
 
         @pl.when(s > 0)
@@ -212,33 +218,56 @@
 
         from_left = piece(row_s, (x + 3) % RING, core, u)
         from_right = piece(row_s, (x + 1) % RING, core, u)
-        part = kv.at[0, from_left]
-        landed(part, right_recv.at[q, 0])
-        remote(part, part, right_send.at[q, 2], right_recv.at[q, 2], right).start()
-        part = kv.at[1, from_right]
-        landed(part, left_recv.at[q, 1])
-        remote(part, part, left_send.at[q, 2], left_recv.at[q, 2], left).start()
-        landed(kv.at[1, from_left], right_recv.at[q, 1])
-        part = kv.at[:, from_left]
-        remote(part, part, core_send.at[q, 1], core_recv.at[q, 1], other_core).start()
-        landed(kv.at[0, from_right], left_recv.at[q, 0])
-        part = kv.at[:, from_right]
-        remote(part, part, core_send.at[q, 2], core_recv.at[q, 2], other_core).start()
+        def k_from_left():
+            landed(kv.at[0, from_left], right_recv.at[q, 0])
+
+        def k_to_right():
+            part = kv.at[0, from_left]
+            remote(part, part, right_send.at[q, 2], right_recv.at[q, 2], right).start()
+
+        def v_from_right():
+            part = kv.at[1, from_right]
+            landed(part, left_recv.at[q, 1])
+            remote(part, part, left_send.at[q, 2], left_recv.at[q, 2], left).start()
+
+        def left_to_core():
+            landed(kv.at[1, from_left], right_recv.at[q, 1])
+            part = kv.at[:, from_left]
+            remote(part, part, core_send.at[q, 1], core_recv.at[q, 1], other_core).start()
+
+        def right_to_core():
+            landed(kv.at[0, from_right], left_recv.at[q, 0])
+            part = kv.at[:, from_right]
+            remote(part, part, core_send.at[q, 2], core_recv.at[q, 2], other_core).start()
+
+        pl.when((s > 0) | (x > 0))(k_from_left)
+        pl.when((s > 0) | (x == 1) | (x == 2))(k_to_right)
+        pl.when((s > 0) | (x == 3) | (x == 0))(v_from_right)
+        pl.when((s > 0) | (x > 0))(left_to_core)
+        pl.when((s > 0) | (x == 3))(right_to_core)
 
     def opposite(s, u):
         far, q = piece(row - s, (x + 2) % RING, core, u), u * RING + s
-        landed(kv.at[0, far], right_recv.at[q, 2])
-        landed(kv.at[1, far], left_recv.at[q, 2])
-        part = kv.at[:, far]
-        remote(part, part, core_send.at[q, 3], core_recv.at[q, 3], other_core).start()
+
+        @pl.when((s > 0) | (x > 1))
+        def _():
+            landed(kv.at[0, far], right_recv.at[q, 2])
+            landed(kv.at[1, far], left_recv.at[q, 2])
+            part = kv.at[:, far]
+            remote(part, part, core_send.at[q, 3], core_recv.at[q, 3], other_core).start()
+
+    def from_core(s, n):
+        return (s > 0) | (x >= (0, 1, 3, 2)[n])
 
     def core_landed(s, carry):
         for u in range(2):
             for n, shift in enumerate((0, 3, 1, 2)):
-                landed(
-                    kv.at[:, piece(row - s, (x + shift) % RING, 1 - core, u)],
-                    core_recv.at[u * RING + s, n],
-                )
+                @pl.when(from_core(s, n))
+                def _():
+                    landed(
+                        kv.at[:, piece(row - s, (x + shift) % RING, 1 - core, u)],
+                        core_recv.at[u * RING + s, n],
+                    )
         return carry
 
     def weight_step(n):
@@ -455,10 +484,14 @@
 
         for u in range(2):
             for n in range(3):
-                sent(part, right_send.at[u * RING + s, n])
-                sent(part, left_send.at[u * RING + s, n])
+                to_right = (s > 0) | ((x == 1) | (x == 2) if n == 2 else x < 3)
+                to_left = (s > 0) | (x == 0) | (
+                    x == 3 if n == 2 else (x == 1) & (n == 1)
+                )
+                pl.when(to_right)(lambda: sent(part, right_send.at[u * RING + s, n]))
+                pl.when(to_left)(lambda: sent(part, left_send.at[u * RING + s, n]))
             for n in range(4):
-                sent(own, core_send.at[u * RING + s, n])
+                pl.when(from_core(s, n))(lambda: sent(own, core_send.at[u * RING + s, n]))
         return carry
 
     lax.fori_loop(0, row + 1, ctx_sent, 0)
@@ -540,7 +573,7 @@
         v.reshape(tokens // MASK_BLOCK_SIZE, MASK_BLOCK_SIZE, -1),
         out_weight, vert.transpose(0, 2, 1), slash.transpose(0, 2, 1),
     )
-    rows = 32
+    rows = 16
     row_block = pl.BlockSpec((rows, D), lambda i: (i, 0))
     return pl.pallas_call(
         finish,

time: 164 us -> 165 us (level)
    pallas_call x1, Pallas kernels: 4.16 us -> 6.18 us  [per_device(): pl.pallas_call(finish, grid=(tokens // rows,), out_shape=[jax.ShapeDtypeS...]
where the time goes in v3:
time: 165 us; the launch traced here: 163 us
  Pallas kernels  162 us (98%)
    pallas_call x1, Pallas kernels, per_device(): pl.pallas_call(kernel, out_shape=jax.ShapeDtypeStruct((CHUNKS, tokens, CH...  156 us
    pallas_call x1, Pallas kernels, per_device(): pl.pallas_call(finish, grid=(tokens // rows,), out_shape=[jax.ShapeDtypeS...  6.18 us

profile of v3, /device:TPU:225, one launch (start us, length us, event | category | flops | bytes accessed | tf_op | source)
XLA Modules:
  0.0 163.0 jit_solution(8272720408137294100)
XLA Ops:
  0.6 156.2 %attention_layer.1.stream = f32[4,128,1024]{2,1,0:T(8,128)} custom-call(bf16[128,4096]{1,0:T(8,128)(2,1)} %q_in.1, bf16[2,64,1024]{2,1,0:T(8,128)(2,1)} %bitcast.6, bf16[2,64,1024]{2,1,0:T(8,128)(2,1)} %bitcast.7, bf16[512,4096]{1,0:T(8,128)(2,1)} %w_in.1, s32[1,8,16]{2,1,0:T(8,128)} %bitcast.8, s32[1,4,16]{2,1,0:T(4,128)} %bitcast.9), custom_call_target="tpu_custom_call" | custom-call | flops 6000000000 | bytes 10000000 | tf_op jit(solution)/shard_map/attention_layer/pallas_call | solution.py:540
  156.8 6.2 %residual_norm.1 = (bf16[128,4096]{1,0:T(8,128)(2,1)}, bf16[128,4096]{1,0:T(8,128)(2,1)}) custom-call(f32[4,128,1024]{2,1,0:T(8,128)} %attention_layer.1.stream, bf16[128,4096]{1,0:T(8,128)(2,1)} %residual.1, bf16[32,128]{1,0:T(8,128)(2,1)} %bitcast.5), custom_call_target="tpu_custom_call" | custom-call | tf_op jit(solution)/shard_map/residual_norm/pallas_call | solution.py:578
